TPU v7x, 256 devices: a whole 4x4x8 slice. The times are simulated.
256 devices in a mesh: rec: 32 (over x_lo, z, core), tm: 8 (over y, x_hi).
Axes of the slice: x: 4 (x_hi: 2, x_lo: 2; x = x_hi * 2 + x_lo), y: 4, z: 8, core: 2. Of those that a mesh axis runs over, the one named last changes fastest.
Arguments:
- frames_in: bfloat16 [64, 512, 1536], P('rec', 'tm'), parts along dimension 0, may hold values from -6 to 6
- lengths: int32 [64], P('rec'), parts along dimension 0, may hold values from 128 to 512, as said below
- ln1_gain: float32 [1536], replicated, may hold values from 0.5 to 1.5
- w_qkv: bfloat16 [3, 1536, 1536], P(None, 'tm'), may hold values from -0.15625 to 0.15625
- bias_u: float32 [16, 96], P('tm'), may hold values from -3 to 3
- bias_v: float32 [16, 96], P('tm'), may hold values from -8 to 8
- pos_keys: bfloat16 [1536, 1024], P('tm'), may hold values from -8 to 8
- w_out: bfloat16 [1536, 1536], P('tm'), may hold values from -0.625 to 0.625
- ln2_gain: float32 [1536], replicated, may hold values from 0.5 to 1.5
- w_glu: bfloat16 [2, 1536, 1536], P(None, 'tm'), may hold values from -0.15625 to 0.15625
- depth_kernel: float32 [31, 1536], replicated, may hold values from -1 to 1
- bn_scale: float32 [1536], replicated, may hold values from 0.25 to 1.75
- bn_shift: float32 [1536], replicated, may hold values from -3 to 3
Outputs:
- attended: bfloat16 [64, 512, 1536], P('rec', 'tm'), parts along dimension 0
- conv_out: bfloat16 [64, 512, 1536], P('rec', 'tm'), parts along dimension 0
There are 32 independent parts, one for each index of `rec`. A program takes and returns all parts, laid end to end along the dimension named above; an argument that names none is the same for every part. Nothing has to cross between parts.
Inputs may be any that keep to these rules, and one draw needn't show every extreme that they name: `lengths`: each recording's count of valid frames from its start; in every part one recording is full (512).
All inputs are finite; a program needn't handle non-finite values.
Results may differ from a plain program's by a relative error of at most 0.012.
Values may be sent and summed in bfloat16 or wider, within the bound.
A program may use at most 128 MiB of HBM per device.

v0:
```python
import math

import jax
import jax.numpy as jnp
from jax import lax
from jax.sharding import PartitionSpec as P


def extended(array, sides, width):
    for axis, dim in sides:
        size, length = (lax.axis_size(axis), array.shape[dim])
        up = [(i, (i + 1) % size) for i in range(size - 1)]
        down = [(j, i) for i, j in up]
        last = lax.slice_in_dim(array, length - width, length, axis=dim)
        first = lax.slice_in_dim(array, 0, width, axis=dim)
        before = lax.ppermute(last, axis, up)
        after = lax.ppermute(first, axis, down)
        array = jnp.concatenate([before, array, after], axis=dim)
    return array


def layer_norm(values, gain):
    wide = values.astype(jnp.float32)
    mean = jnp.mean(wide, axis=-1, keepdims=True)
    centered = wide - mean
    variance = jnp.mean(centered * centered, axis=-1, keepdims=True)
    return centered * lax.rsqrt(variance + 1e-05) * gain


def skew_rows(matrix, frames):
    block, width = (matrix.shape[-2], matrix.shape[-1])
    flat = matrix.reshape(matrix.shape[:-2] + (block * width,))
    moved = flat[..., block - 1 : block - 1 + block * (width - 1)]
    return moved.reshape(matrix.shape[:-2] + (block, width - 1))[..., :frames]


def attend(qkv, bias_u, bias_v, pos_keys, length):
    heads, head_dim = bias_u.shape
    frames = qkv.shape[0]
    block = min(512, frames)
    count = frames // block
    scale = 1.0 / math.sqrt(head_dim)
    query = qkv[:, 0].reshape(frames, heads, head_dim)
    keys = qkv[:, 1].reshape(frames, heads, head_dim)
    values = qkv[:, 2].reshape(frames, heads, head_dim)
    position = pos_keys.reshape(heads, head_dim, 2 * frames)
    key_valid = jnp.arange(frames) < length

    def one_block(index):
        start = index * block
        rows = query.astype(jnp.float32)
        query_u = (rows + bias_u).astype(jnp.bfloat16)
        query_v = (rows + bias_v).astype(jnp.bfloat16)
        content = jnp.einsum("bhd,jhd->hbj", query_u, keys, preferred_element_type=jnp.float32)
        window = lax.dynamic_slice_in_dim(position, frames - start - block, frames + block - 1, 2)
        relative = skew_rows(
            jnp.einsum("bhd,hdw->hbw", query_v, window, preferred_element_type=jnp.float32), frames
        )
        scores = (content + relative) * scale
        scores = jnp.where(key_valid[None, None, :], scores, -1e30)
        peak = jnp.max(scores, axis=-1, keepdims=True)
        expd = jnp.exp(scores - peak)
        total = jnp.sum(expd, axis=-1, keepdims=True)
        weights = (expd / total).astype(jnp.bfloat16)
        mixed = jnp.einsum("hbj,jhd->bhd", weights, values, preferred_element_type=jnp.float32)
        return mixed.astype(jnp.bfloat16).reshape(block, heads * head_dim)

    outputs = lax.map(one_block, jnp.arange(count, dtype=jnp.int32))
    return outputs.reshape(frames, heads * head_dim)


def depthwise(padded, kernel, scale_part, shift_part, count):
    summed = jnp.zeros((padded.shape[0], count, padded.shape[2]), jnp.float32)
    for offset in range(kernel.shape[0]):
        summed = summed + padded[:, offset : offset + count].astype(jnp.float32) * kernel[offset]
    shifted = summed * scale_part + shift_part
    return shifted * jax.nn.sigmoid(shifted)


def on_device(
    frames_in,
    lengths,
    ln1_gain,
    w_qkv,
    bias_u,
    bias_v,
    pos_keys,
    w_out,
    ln2_gain,
    w_glu,
    depth_kernel,
    bn_scale,
    bn_shift,
):
    recordings, frames_dev, width_all = frames_in.shape
    device_rank = lax.axis_index("tm")
    half = depth_kernel.shape[0] // 2
    normed = layer_norm(frames_in, ln1_gain).astype(jnp.bfloat16)
    own_qkv = jnp.einsum(
        "rfd,kcd->rfkc",
        normed,
        lax.all_gather(w_qkv, "tm", axis=1, tiled=True),
        preferred_element_type=jnp.float32,
    ).astype(jnp.bfloat16)
    regrouped = lax.all_to_all(own_qkv, "tm", split_axis=3, concat_axis=1, tiled=True)
    head_outputs = jnp.stack(
        [
            attend(regrouped[index], bias_u, bias_v, pos_keys, lengths[index])
            for index in range(recordings)
        ]
    )
    by_frames = lax.all_to_all(head_outputs, "tm", split_axis=1, concat_axis=2, tiled=True)
    projected = jnp.einsum(
        "rfc,cd->rfd",
        by_frames,
        lax.all_gather(w_out, "tm", axis=0, tiled=True),
        preferred_element_type=jnp.float32,
    )
    attended = (frames_in.astype(jnp.float32) + projected).astype(jnp.bfloat16)
    normed2 = layer_norm(attended, ln2_gain).astype(jnp.bfloat16)
    piece = lax.all_gather(w_glu, "tm", axis=1, tiled=True)
    first = jnp.einsum("rfd,cd->rfc", normed2, piece[0], preferred_element_type=jnp.float32)
    second = jnp.einsum("rfd,cd->rfc", normed2, piece[1], preferred_element_type=jnp.float32)
    gated = first * jax.nn.sigmoid(second)
    positions = device_rank * frames_dev + jnp.arange(frames_dev)
    gated = jnp.where(positions[None, :, None] < lengths[:, None, None], gated, 0.0).astype(
        jnp.bfloat16
    )
    padded = extended(gated, (("tm", 1),), half)
    conv_out = depthwise(padded, depth_kernel, bn_scale, bn_shift, frames_dev).astype(jnp.bfloat16)
    return (attended, conv_out)


def solution(mesh):
    placed = (
        P("rec", "tm", None),
        P("rec"),
        P(),
        P(None, "tm", None),
        P("tm", None),
        P("tm", None),
        P("tm", None),
        P("tm", None),
        P(),
        P(None, "tm", None),
        P(),
        P(),
        P(),
    )
    return jax.shard_map(
        on_device,
        mesh=mesh,
        in_specs=placed,
        out_specs=(P("rec", "tm", None), P("rec", "tm", None)),
        check_vma=False,
    )
```

profile of v0, /device:TPU:1, one launch (start us, length us, event | category | flops | bytes accessed | tf_op | source)
XLA Modules:
  0.0 422.8 jit_solution(11968692053099657849)
XLA Ops:
  9.8 168.4 %all-gather.4.cloned.1.call-done = bf16[3,1536,1536]{2,1,0:T(8,128)(2,1)} async-done(((bf16[3,192,1536]{2,1,0:T(8,128)(2,1)}), bf16[3,1536,1536]{2,1,0:T(8,128)(2,1)}) %all-gather.4.cloned.1.call-update) | async-done | bytes 14155792 | tf_op jit(solution)/shard_map/all_gather | solution.py:102
  178.2 10.8 %fusion.8 = bf16[2,64,3,1536]{3,1,2,0:T(8,128)(2,1)} fusion(bf16[3,1536,1536]{2,1,0:T(8,128)(2,1)} %all-gather.4.cloned.1.call-done, bf16[2,64,1536]{2,1,0:T(8,128)(2,1)S(1)} %copy-done, f32[1536]{0:T(1024)S(1)} %copy-done.10, f32[2,64]{1,0:T(2,128)S(1)} %add_rsqrt_fusion.1, f32[2,64]{1,0:T(2,128)S(1)} %broadcast_multiply_fusion.1), kind=kOutput, calls=%fused_computation.10 | convolution fusion | flops 1813512192 | bytes 15735808 | tf_op jit(solution)/shard_map/rfd,kcd->rfkc/dot_general | solution.py:99
  189.0 6.4 %copy.80 = bf16[2,64,3,1536]{1,0,2,3:T(2,128)(2,1)S(1)} copy(bf16[2,64,3,1536]{3,1,2,0:T(8,128)(2,1)} %fusion.8) | data formatting | bytes 2359296 | tf_op jit(solution)/shard_map/convert_element_type | solution.py:104
  195.4 2.8 reshape.191
  198.2 4.5 %all-to-all-start = ((bf16[8,2,36864]{2,1,0:T(2,128)(2,1)}), bf16[8,2,36864]{2,1,0:T(2,128)(2,1)}, u32[]{:S(2)}, u32[]{:S(2)}) async-start(bf16[8,2,36864]{2,1,0:T(2,128)(2,1)} %reshape.191), calls=%async_computation | async-start | bytes 2359296 | tf_op jit(solution)/shard_map/all_to_all | solution.py:105
  204.7 18.2 %all-to-all-done = bf16[8,2,36864]{2,1,0:T(2,128)(2,1)} async-done(((bf16[8,2,36864]{2,1,0:T(2,128)(2,1)}), bf16[8,2,36864]{2,1,0:T(2,128)(2,1)}, u32[]{:S(2)}, u32[]{:S(2)}) %all-to-all-start) | async-done | bytes 1179680 | tf_op jit(solution)/shard_map/all_to_all | solution.py:105
  222.9 3.3 reshape.192
  226.2 3.8 copy.81
  232.5 2.7 fusion.73
  235.2 9.7 %reshape.149 = f32[2,523776]{1,0:T(2,128)} reshape(f32[2,512,1023]{2,1,0:T(8,128)} %fusion.73) | data formatting | bytes 8380416 | tf_op jit(solution)/shard_map/while/body/eval_jaxpr/reshape | solution.py:32
  245.0 7.6 %slice.357 = f32[2,523264]{1,0:T(2,128)} slice(f32[2,523776]{1,0:T(2,128)} %reshape.149), slice={[0:2], [511:523775]} | slice | bytes 8372224 | tf_op jit(solution)/shard_map/while/body/eval_jaxpr/slice | solution.py:33
  252.6 9.9 %reshape.150 = f32[2,512,1022]{2,1,0:T(8,128)} reshape(f32[2,523264]{1,0:T(2,128)} %slice.357) | data formatting | bytes 8372224 | tf_op jit(solution)/shard_map/while/body/eval_jaxpr/reshape | solution.py:34
  264.2 1.9 copy.100
  266.0 1.8 copy.84
  267.8 1.8 copy.82
  269.5 2.4 multiply_select_fusion.1
  274.2 2.6 copy.92
  277.7 2.7 fusion.71
  280.5 10.3 %reshape.151 = f32[2,523776]{1,0:T(2,128)} reshape(f32[2,512,1023]{2,1,0:T(8,128)} %fusion.71) | data formatting | bytes 8380416 | tf_op jit(solution)/shard_map/while/body/eval_jaxpr/reshape | solution.py:32
  290.7 7.5 %slice.363 = f32[2,523264]{1,0:T(2,128)} slice(f32[2,523776]{1,0:T(2,128)} %reshape.151), slice={[0:2], [511:523775]} | slice | bytes 8372224 | tf_op jit(solution)/shard_map/while/body/eval_jaxpr/slice | solution.py:33
  298.2 10.0 %reshape.152 = f32[2,512,1022]{2,1,0:T(8,128)} reshape(f32[2,523264]{1,0:T(2,128)} %slice.363) | data formatting | bytes 8372224 | tf_op jit(solution)/shard_map/while/body/eval_jaxpr/reshape | solution.py:34
  309.9 1.9 copy.102
  312.7 2.2 multiply_select_fusion
  317.0 2.1 pad_maximum_fusion
  319.0 3.7 all-to-all-start.1
  323.2 16.8 %all-to-all-done.1 = bf16[2,512,192]{2,0,1:T(2,128)(2,1)S(1)} async-done(((bf16[2,512,192]{2,0,1:T(2,128)(2,1)}), bf16[2,512,192]{2,0,1:T(2,128)(2,1)S(1)}, u32[]{:S(2)}, u32[]{:S(2)}) %all-to-all-start.1) | async-done | bytes 393248 | tf_op jit(solution)/shard_map/all_to_all | solution.py:112
  340.8 3.3 convert_reduce_fusion.1
  344.3 51.1 %all-gather.8.cloned.1.call-done = bf16[2,1536,1536]{2,1,0:T(8,128)(2,1)} async-done(((bf16[2,192,1536]{2,1,0:T(8,128)(2,1)}), bf16[2,1536,1536]{2,1,0:T(8,128)(2,1)}) %all-gather.8.cloned.1.call-update) | async-done | bytes 9437200 | tf_op jit(solution)/shard_map/all_gather | solution.py:121
  395.4 4.2 fusion.23
  402.2 2.2 collective-permute-start
  406.0 5.3 %collective-permute-done.1 = bf16[2,15,1536]{2,1,0:T(8,128)(2,1)S(1)} collective-permute-done((bf16[2,15,1536]{2,1,0:T(8,128)(2,1)S(1)}, bf16[2,15,1536]{2,1,0:T(8,128)(2,1)S(1)}, u32[]{:S(2)}, u32[]{:S(2)}) %collective-permute-start.1) | collective-permute-done | bytes 92192 | tf_op jit(solution)/shard_map/ppermute | solution.py:17
  411.4 4.7 %multiply_convert_fusion = bf16[2,64,1536]{2,1,0:T(8,128)(2,1)} fusion(bf16[2,64,1536]{2,1,0:T(8,128)(2,1)S(1)} %fusion.19, bf16[2,15,1536]{2,1,0:T(8,128)(2,1)S(1)} %collective-permute-done.1, bf16[2,15,1536]{2,1,0:T(8,128)(2,1)S(1)} %collective-permute-done, f32[1536]{0:T(1024)S(1)} %copy-done.11, f32[1536]{0:T(1024)S(1)} %copy-done.12, ...), kind=kLoop, calls=%fused_computation.70 | loop fusion | flops 37158912 | bytes 1173504 | tf_op jit(solution)/shard_map/convert_element_type | solution.py:130
  (80 shorter events, 22.0 us)
Async XLA Ops:
  7.2 2.2 copy-start
  7.2 171.1 %copy-start.10 = (f32[1536]{0:T(1024)S(1)}, f32[1536]{0:T(1024)}, u32[]{:S(2)}) copy-start(f32[1536]{0:T(1024)} %param.15) | copy-start | bytes 18436
  7.2 171.0 %all-gather.4.cloned.1.call-start = ((), (), s32[]{:S(2)}) async-start(), calls=%async_computation.2 | async-start | bytes 15925248 | tf_op jit(solution)/shard_map/all_gather | solution.py:102
  7.9 332.9 %all-gather.6.cloned.1.call-start = ((), (), s32[]{:S(2)}) async-start(), calls=%async_computation.3 | async-start | bytes 5308416 | tf_op jit(solution)/shard_map/all_gather | solution.py:116
  8.7 386.8 %all-gather.8.cloned.1.call-start = ((), (), s32[]{:S(2)}) async-start(), calls=%async_computation.4 | async-start | bytes 10616832 | tf_op jit(solution)/shard_map/all_gather | solution.py:121
  195.4 7.4 %copy-start.15 = (s32[2]{0:T(128)S(1)}, s32[2]{0:T(128)}, u32[]{:S(2)}) copy-start(s32[2]{0:T(128)} %param.14) | copy-start | bytes 28
  198.2 24.7 %all-to-all-start = ((bf16[8,2,36864]{2,1,0:T(2,128)(2,1)}), bf16[8,2,36864]{2,1,0:T(2,128)(2,1)}, u32[]{:S(2)}, u32[]{:S(2)}) async-start(bf16[8,2,36864]{2,1,0:T(2,128)(2,1)} %reshape.191), calls=%async_computation | async-start | bytes 2359296 | tf_op jit(solution)/shard_map/all_to_all | solution.py:105
  229.9 2.5 copy-start.3
  229.9 2.5 copy-start.13
  262.6 1.6 slice-start
  264.2 5.4 %copy-start.14 = (f32[2,96]{1,0:T(2,128)S(1)}, f32[2,96]{1,0:T(2,128)}, u32[]{:S(2)}) copy-start(f32[2,96]{1,0:T(2,128)} %param.17) | copy-start | bytes 2308
  271.9 0.9 copy-start.7
  274.2 3.5 copy-start.4
  308.3 1.6 slice-start.1
  309.9 1.9 copy-start.6
  309.9 2.0 copy-start.5
  314.9 0.9 copy-start.8
  315.8 1.1 copy-start.1
  316.5 6.3 %copy-start.9 = (f32[31,1536]{1,0:T(8,128)S(1)}, f32[31,1536]{1,0:T(8,128)}, u32[]{:S(2)}) copy-start(f32[31,1536]{1,0:T(8,128)} %param.23) | copy-start | bytes 571396
  319.0 20.9 %all-to-all-start.1 = ((bf16[2,512,192]{2,0,1:T(2,128)(2,1)}), bf16[2,512,192]{2,0,1:T(2,128)(2,1)S(1)}, u32[]{:S(2)}, u32[]{:S(2)}) async-start(bf16[2,512,192]{2,0,1:T(2,128)(2,1)} %pad_maximum_fusion), calls=%async_computation.1 | async-start | bytes 1048576 | tf_op jit(solution)/shard_map/all_to_all | solution.py:112
  340.7 54.7 %copy-start.17 = (f32[1536]{0:T(1024)S(1)}, f32[1536]{0:T(1024)}, u32[]{:S(2)}) copy-start(f32[1536]{0:T(1024)} %param.21) | copy-start | bytes 18436
  344.0 55.6 %copy-start.2 = (bf16[2,64,1536]{2,1,0:T(8,128)(2,1)}, bf16[2,64,1536]{2,1,0:T(8,128)(2,1)S(1)}, u32[]{:S(2)}) copy-start(bf16[2,64,1536]{2,1,0:T(8,128)(2,1)S(1)} %get-tuple-element.100) | copy-start | bytes 1179652
  395.4 5.1 %copy-start.16 = (bf16[2,1536,1536]{2,1,0:T(8,128)(2,1)S(1)}, bf16[2,1536,1536]{2,1,0:T(8,128)(2,1)}, u32[]{:S(2)}) copy-start(bf16[2,1536,1536]{2,1,0:T(8,128)(2,1)} %all-gather.8.cloned.1.call-done) | copy-start | bytes 28311556
  400.5 10.8 %copy-start.11 = (f32[1536]{0:T(1024)S(1)}, f32[1536]{0:T(1024)}, u32[]{:S(2)}) copy-start(f32[1536]{0:T(1024)} %param.25) | copy-start | bytes 18436
  400.5 10.8 %copy-start.12 = (f32[1536]{0:T(1024)S(1)}, f32[1536]{0:T(1024)}, u32[]{:S(2)}) copy-start(f32[1536]{0:T(1024)} %param.24) | copy-start | bytes 18436
  402.2 3.8 collective-permute-start
  404.4 6.9 %collective-permute-start.1 = (bf16[2,15,1536]{2,1,0:T(8,128)(2,1)S(1)}, bf16[2,15,1536]{2,1,0:T(8,128)(2,1)S(1)}, u32[]{:S(2)}, u32[]{:S(2)}) collective-permute-start(bf16[2,15,1536]{2,1,0:T(8,128)(2,1)S(1)} %get-tuple-element.96), channel_id=1, source_target_pairs={{1,0},{2,1},{3,2},{4,3},{5,4},{6,5},{7,6},{9,8},{10,9},{11,10},{12... | collective-permute-start | bytes 276488 | tf_op jit(solution)/shard_map/ppermute | solution.py:17
Sparse Core Ops, SparseCore 0:
  10.6 167.5 all-gather.3
  180.8 86.7 all-gather.5
  270.3 125.1 all-gather.7
where the time goes:
time: 429 us; the launch traced here: 423 us
  waiting for transfers between devices  262 us (61%)
  local copies, waits for them, and re-layouts  93 us (22%)
  matrix products  31.9 us (7%)
  between operations  14.4 us (3%)
  starting transfers between devices  11.8 us (3%)
  other arithmetic  9.71 us (2%)
    all_gather x1, waiting for transfers between devices, on_device(): lax.all_gather(w_qkv, 'tm', axis=1, tiled=True)  168 us
    all_gather x1, waiting for transfers between devices, on_device(): piece = lax.all_gather(w_glu, 'tm', axis=1, tiled=True)  51.1 us
    reshape x2, local copies, waits for them, and re-layouts, skew_rows(): flat = matrix.reshape(matrix.shape[:-2] + (block * width,))  20 us
    reshape x2, local copies, waits for them, and re-layouts, skew_rows(): return moved.reshape(matrix.shape[:-2] + (block, width - 1))[..., :frames]  20 us
    all_to_all x1, waiting for transfers between devices, on_device(): lax.all_to_all(own_qkv, 'tm', split_axis=3, concat_axis=1, tiled=True)  18.2 us
    all_to_all x1, waiting for transfers between devices, on_device(): lax.all_to_all(head_outputs, 'tm', split_axis=1, concat_axis=2, tiled=True)  16.8 us
    slice x2, local copies, waits for them, and re-layouts, skew_rows(): moved = flat[..., block - 1:block - 1 + block * (width - 1)]  15.1 us
    unnamed x42, local copies, waits for them, and re-layouts  12 us
  transfers between devices with their start and end apart: 7, of which 6 were waited for; matrix products, arithmetic and copies ran while one was open for 28% of the time, Pallas kernels for 0%

commit v1 on v0

v1 whole, which is shorter than its diff:
```python
import functools
import math

import jax
import jax.numpy as jnp
from jax import lax
from jax.experimental import pallas as pl
from jax.experimental.pallas import tpu as pltpu
from jax.sharding import PartitionSpec as P

MESH = pl.DeviceIdType.MESH
F32, BF16 = jnp.float32, jnp.bfloat16
PEERS = 8
Z_CHIPS = 8
FD = 64
FRAMES = 512
D = 1536
CH = 192
DH = 96
TAPS = 31
NT = (((1,), (1,)), ((), ()))
NN = (((1,), (0,)), ((), ()))
SCALE2 = math.log2(math.e) / math.sqrt(DH)


def dot(a, b, dims=NN):
    return lax.dot_general(a, b, dims, preferred_element_type=F32)


def norm_rows(values, gain):
    mean = jnp.mean(values, axis=-1, keepdims=True)
    centered = values - mean
    variance = jnp.mean(centered * centered, axis=-1, keepdims=True)
    return (centered * lax.rsqrt(variance + 1e-05) * gain).astype(BF16)


def sigmoid(v):
    return 1.0 / (1.0 + jnp.exp(-v))


def kernel(
    frames_hbm, lengths, gain1, w_qkv_hbm, bias_u, bias_v, pos_hbm, w_out_hbm, gain2, w_glu_hbm,
    taps_ref, scale_ref, shift_ref,
    attended, conv_out,
    x, nrm, n2, wq, wg, wo, pos, qkv, vext, hs, hb, gp, cs, cb, bias_s, taps_s, bn_s,
    local_sem, ag_send, ag_recv, aa_send, aa_recv, wo_send, wo_recv,
):
    rec, me = lax.axis_index("rec"), lax.axis_index("tm")
    y, xh = me // 2, lax.rem(me, 2)
    core, z = lax.rem(rec, 2), lax.rem(rec // 2, Z_CHIPS)
    x_lo = rec // (2 * Z_CHIPS)

    def rec_of(zz, cc):
        return (x_lo * Z_CHIPS + lax.rem(zz + Z_CHIPS, Z_CHIPS)) * 2 + cc

    def slot(dy, flip):
        return lax.rem(y + dy, 4) * 2 + (1 - xh if flip else xh)

    s_x, s_up, s_dn, s_far = slot(0, True), slot(1, False), slot(3, False), slot(2, False)
    s_upx, s_dnx, s_farx = slot(1, True), slot(3, True), slot(2, True)
    z_up, z_dn, sibling = rec_of(z + 1, core), rec_of(z - 1, core), rec_of(z, 1 - core)

    def remote(src, dst, send, recv, device):
        return pltpu.make_async_remote_copy(
            src_ref=src, dst_ref=dst, send_sem=send, recv_sem=recv, device_id=device,
            device_id_type=MESH,
        )

    quarter = lax.rem(z, 4)
    wo_rows = pl.ds(pl.multiple_of(quarter * 48, 16), 48)
    wo_cols = pl.ds(pl.multiple_of(core * 768, 128), 768)
    loads = [
        (frames_hbm.at[0], x.at[0]),
        (frames_hbm.at[1], x.at[1]),
        (w_out_hbm.at[wo_rows, wo_cols], wo.at[me, wo_rows, wo_cols]),
        (w_qkv_hbm.at[0, pl.ds(0, DH)], wq.at[pl.ds(0, DH)]),
        (w_qkv_hbm.at[0, pl.ds(DH, DH)], wq.at[pl.ds(128, DH)]),
        (w_qkv_hbm.at[1, pl.ds(0, DH)], wq.at[pl.ds(256, DH)]),
        (w_qkv_hbm.at[1, pl.ds(DH, DH)], wq.at[pl.ds(384, DH)]),
        (w_qkv_hbm.at[2], wq.at[pl.ds(512, CH)]),
        (pos_hbm.at[pl.ds(0, DH)], pos.at[0, pl.ds(0, DH)]),
        (pos_hbm.at[pl.ds(DH, DH)], pos.at[1, pl.ds(0, DH)]),
        (w_glu_hbm.at[0], wg.at[pl.ds(0, CH)]),
        (w_glu_hbm.at[1], wg.at[pl.ds(256, CH)]),
    ]
    loads = [pltpu.make_async_copy(s, d, local_sem.at[i]) for i, (s, d) in enumerate(loads)]
    for load in loads:
        load.start()

    barrier = pltpu.get_barrier_semaphore()
    for step in range(1, PEERS):
        pl.semaphore_signal(
            barrier, inc=1, device_id=(rec, lax.rem(me + step, PEERS)), device_id_type=MESH
        )
    for other in (z_up, z_dn, sibling):
        pl.semaphore_signal(barrier, inc=1, device_id=(other, me), device_id_type=MESH)

    def ag(which, buf, r, index, arriving=False):
        low, high = (pl.ds(0, 32),), (pl.ds(32, 32),)
        plan = [
            (me, (), s_x, s_x),
            (me, (), s_up, s_dn),
            (me, (), s_dn, s_up),
            (s_x, (), s_up, s_dnx),
            (s_x, (), s_dn, s_upx),
            (s_dn, low, s_up, s_far),
            (s_up, high, s_dn, s_far),
            (s_far, low, s_x, s_farx),
            (s_far, high, s_x, s_farx),
        ]
        src, rows, target, landing = plan[index]
        sems = (ag_send.at[which, r, index], ag_recv.at[which, r, index])
        part = buf.at[(r, landing if arriving else src) + rows]
        return remote(part, part, *sems, (rec, target))

    def ag_start(which, buf, r, *indices):
        for index in indices:
            ag(which, buf, r, index).start()

    def ag_wait(which, buf, r, *indices):
        for index in indices:
            ag(which, buf, r, index, True).wait_recv()

    def ag_first(which, buf, r):
        ag_start(which, buf, r, 0, 1, 2)

    def ag_second(which, buf, r):
        ag_wait(which, buf, r, 1)
        ag_start(which, buf, r, 5)
        ag_wait(which, buf, r, 2)
        ag_start(which, buf, r, 6)
        ag_wait(which, buf, r, 0)
        ag_start(which, buf, r, 3, 4)

    def ag_third(which, buf, r):
        ag_wait(which, buf, r, 5)
        ag_start(which, buf, r, 7)
        ag_wait(which, buf, r, 6)
        ag_start(which, buf, r, 8)

    def ag_finish(which, buf, r):
        ag_wait(which, buf, r, 3, 4, 7, 8)

    def aa(which, out, into, r, step, arriving=False):
        to, source = lax.rem(me + step, PEERS), lax.rem(me + PEERS - step, PEERS)
        sems = (aa_send.at[which, r, step], aa_recv.at[which, r, step])
        return remote(out.at[r, to], into.at[r, source if arriving else me], *sems, (rec, to))

    def aa_start(which, out, into, r):
        for step in range(1, PEERS):
            aa(which, out, into, r, step).start()
        into[r, me] = out[r, me]

    def aa_wait(which, out, into, r):
        for step in range(1, PEERS):
            aa(which, out, into, r, step, True).wait_recv()

    def wo_set(q, c, half=None):
        width = 768 if half is None else 384
        start = c * 768 + (0 if half is None else half * 384)
        return wo.at[
            :,
            pl.ds(pl.multiple_of(lax.rem(q + 4, 4) * 48, 16), 48),
            pl.ds(pl.multiple_of(start, 128), width),
        ]

    def wo_copy(index, arriving=False):
        sems = (wo_send.at[index], wo_recv.at[index])
        if index < 7:
            step = index + 1
            to, source = lax.rem(me + step, PEERS), lax.rem(me + PEERS - step, PEERS)
            mine = wo.at[me, wo_rows, wo_cols]
            landed = wo.at[source, wo_rows, wo_cols]
            device = (rec, to)
        elif index < 11:
            q_sent, half, q_land, to = [
                (quarter, None, quarter - 1, z_up),
                (quarter, None, quarter + 1, z_dn),
                (quarter - 1, 0, quarter - 2, z_up),
                (quarter + 1, 1, quarter + 2, z_dn),
            ][index - 7]
            mine, landed = wo_set(q_sent, core, half), wo_set(q_land, core, half)
            device = (to, me)
        else:
            q, half = [
                (quarter, None), (quarter - 1, None), (quarter + 1, None),
                (quarter - 2, 0), (quarter + 2, 1),
            ][index - 11]
            mine, landed = wo_set(q, core, half), wo_set(q, 1 - core, half)
            device = (sibling, me)
        part = landed if arriving else mine
        return remote(part, part, *sems, device)

    def wo_start(*indices):
        for index in indices:
            wo_copy(index).start()

    def wo_wait(*indices):
        for index in indices:
            wo_copy(index, True).wait_recv()

    def first_norm(r):
        nrm[r, me] = norm_rows(x[r].astype(F32), gain1[...])

    def project(r):
        rows = nrm.at[r]

        @pl.loop(0, 3)
        def _(n):
            cols = pl.ds(pl.multiple_of(n * 256, 256), 256)
            part = dot(rows[...].reshape(FRAMES, D), wq[cols, :], NT)
            qkv[:, cols] = part.astype(BF16)

        v = qkv[:, pl.ds(512, 256)].astype(F32)
        lane = lax.broadcasted_iota(jnp.int32, v.shape, 1)
        ones = jnp.where(lane == CH, 1.0, 0.0)
        vext[0] = jnp.where(lane < DH, v, ones).astype(BF16)
        vext[1] = jnp.where((lane >= DH) & (lane < CH), v, ones).astype(BF16)

    def attend(r):
        valid = lax.broadcasted_iota(jnp.int32, (128, FRAMES), 1) < lengths[r]

        @pl.loop(0, 4)
        def _(block):
            mixed = []
            for h in range(2):
                q = qkv[pl.ds(pl.multiple_of(block * 128, 128), 128), pl.ds(h * 128, 128)].astype(F32)
                query_u = (q + bias_s[0, pl.ds(h, 1), :]).astype(BF16)
                query_v = (q + bias_s[1, pl.ds(h, 1), :]).astype(BF16)
                content = dot(query_u, qkv[:, pl.ds(256 + h * 128, 128)], NT)
                window = pos[h, :, pl.ds(pl.multiple_of(384 - block * 128, 128), 640)]
                relative = dot(query_v, window)
                relative = pltpu.roll(relative, 513, 1, stride=1, stride_axis=0)[:, :FRAMES]
                scores = jnp.where(valid, content + relative, -1e30)
                peak = jnp.max(scores, axis=-1, keepdims=True)
                expd = jnp.exp2((scores - peak) * SCALE2).astype(BF16)
                out = dot(expd, vext[h])
                mixed.append(out / out[:, CH : CH + 1])
            lane = lax.broadcasted_iota(jnp.int32, mixed[0].shape, 1)
            both = jnp.where(lane < DH, mixed[0], mixed[1])[:, :CH].astype(BF16)
            hs[r, 2 * block] = both[:FD]
            hs[r, 2 * block + 1] = both[FD:]

    def out_project(r):
        heads = jnp.concatenate([hb[r, s] for s in range(PEERS)], axis=-1)
        for n in range(3):
            cols = pl.ds(n * 512, 512)
            part = dot(heads, wo[:, :, cols].reshape(D, 512))
            attended[r, :, cols] = (x[r, :, cols].astype(F32) + part).astype(BF16)
        n2[r, me] = norm_rows(attended[r].astype(F32), gain2[...])

    def glu(r):
        @pl.loop(0, 4)
        def _(block):
            rows = n2[r, pl.ds(block * 2, 2)].reshape(128, D)
            both = dot(rows, wg[...], NT)
            gated = both[:, :256] * sigmoid(both[:, 256:])
            frame = block * 128 + lax.broadcasted_iota(jnp.int32, gated.shape, 0)
            gated = jnp.where(frame < lengths[r], gated, 0.0).astype(BF16).astype(F32)
            at = pl.ds(pl.multiple_of(16 + block * 128, 16), 128)
            gp[0, at, :] = gated[:, :128]
            gp[1, at, :] = gated[:, 128:]

    def conv(r):
        @pl.loop(0, PEERS)
        def _(block):
            for c in range(2):
                total = jnp.zeros((FD, 128), F32)
                for t in range(TAPS):
                    total += gp[c, pl.ds(block * FD + t + 1, FD), :] * taps_s[c, pl.ds(t, 1), :]
                s = total * bn_s[0, pl.ds(c, 1), :] + bn_s[1, pl.ds(c, 1), :]
                out = (s * sigmoid(s)).astype(BF16)
                if c == 0:
                    cs[r, block, :, pl.ds(0, 128)] = out
                else:
                    cs[r, block, :, pl.ds(128, 64)] = out[:, :64]

    def conv_finish(r):
        conv_out[r] = jnp.concatenate([cb[r, s] for s in range(PEERS)], axis=-1)

    def prepare():
        for start in (96, 224, 352, 480):
            wq[pl.ds(start, 32), :] = jnp.zeros((32, D), BF16)
        wq[pl.ds(704, 64), :] = jnp.zeros((64, D), BF16)
        for start in (192, 448):
            wg[pl.ds(start, 64), :] = jnp.zeros((64, D), BF16)
        for h in range(2):
            pos[h, pl.ds(DH, 32), :] = jnp.zeros((32, 2 * FRAMES), BF16)
        bias_s[...] = jnp.zeros_like(bias_s)
        bias_s[0, pl.ds(0, 2), pl.ds(0, DH)] = bias_u[...]
        bias_s[1, pl.ds(0, 2), pl.ds(0, DH)] = bias_v[...]
        for c in range(2):
            gp[c, pl.ds(0, 16), :] = jnp.zeros((16, 128), F32)
            gp[c, pl.ds(16 + FRAMES, 16), :] = jnp.zeros((16, 128), F32)
        odd = jnp.full((1, 256), xh, jnp.int32) == 1
        window = pl.ds(pl.multiple_of((3 * me) // 2 * 128, 128), 256)

        def mine(ref, count):
            part = ref[:, window]
            moved = pltpu.roll(part, 192, 1)
            return jnp.where(jnp.broadcast_to(odd, (count, 256)), moved, part)

        taps = mine(taps_ref, TAPS)
        scale, shift = mine(scale_ref, 1), mine(shift_ref, 1)
        for c in range(2):
            cols = slice(c * 128, c * 128 + 128)
            taps_s[c, pl.ds(0, TAPS), :] = taps[:, cols]
            bn_s[0, pl.ds(c, 1), :] = scale[:, cols]
            bn_s[1, pl.ds(c, 1), :] = shift[:, cols]

    loads[0].wait()
    first_norm(0)
    pl.semaphore_wait(barrier, PEERS - 1 + 3)
    ag_first(0, nrm, 0)
    loads[2].wait()
    wo_start(*range(7))
    loads[1].wait()
    first_norm(1)
    prepare()
    ag_second(0, nrm, 0)
    ag_first(0, nrm, 1)
    ag_third(0, nrm, 0)
    wo_wait(*range(7))
    wo_start(7, 8, 11)
    ag_finish(0, nrm, 0)
    for load in loads[3:]:
        load.wait()
    project(0)
    ag_second(0, nrm, 1)
    attend(0)
    aa_start(0, hs, hb, 0)
    ag_third(0, nrm, 1)
    wo_wait(7)
    wo_start(9, 12)
    wo_wait(8)
    wo_start(10, 13)
    ag_finish(0, nrm, 1)
    project(1)
    attend(1)
    aa_start(0, hs, hb, 1)
    wo_wait(9, 10)
    wo_start(14, 15)
    aa_wait(0, hs, hb, 0)
    wo_wait(*range(11, 16))
    out_project(0)
    ag_first(1, n2, 0)
    aa_wait(0, hs, hb, 1)
    out_project(1)
    ag_second(1, n2, 0)
    ag_first(1, n2, 1)
    ag_third(1, n2, 0)
    ag_finish(1, n2, 0)
    ag_second(1, n2, 1)
    glu(0)
    conv(0)
    aa_start(1, cs, cb, 0)
    ag_third(1, n2, 1)
    ag_finish(1, n2, 1)
    glu(1)
    conv(1)
    aa_start(1, cs, cb, 1)
    aa_wait(1, cs, cb, 0)
    conv_finish(0)
    aa_wait(1, cs, cb, 1)
    conv_finish(1)

    for index in range(16):
        wo_copy(index).wait_send()
    for r in range(2):
        for index in range(9):
            ag(0, nrm, r, index).wait_send()
            ag(1, n2, r, index).wait_send()
        for step in range(1, PEERS):
            aa(0, hs, hb, r, step).wait_send()
            aa(1, cs, cb, r, step).wait_send()


def on_device(
    frames_in, lengths, ln1_gain, w_qkv, bias_u, bias_v, pos_keys, w_out, ln2_gain, w_glu,
    depth_kernel, bn_scale, bn_shift,
):
    any_space, vmem = pl.BlockSpec(memory_space=pl.ANY), pl.BlockSpec(memory_space=pltpu.VMEM)
    smem = pl.BlockSpec(memory_space=pltpu.SMEM)
    gathered = pltpu.VMEM((2, PEERS, FD, D), BF16)
    exchanged = pltpu.VMEM((2, PEERS, FD, CH), BF16)
    dma = pltpu.SemaphoreType.DMA
    return pl.pallas_call(
        kernel,
        out_shape=[jax.ShapeDtypeStruct(frames_in.shape, BF16)] * 2,
        in_specs=[
            any_space, smem, vmem, any_space, vmem, vmem, any_space, any_space, vmem, any_space,
            vmem, vmem, vmem,
        ],
        out_specs=[vmem, vmem],
        scratch_shapes=[
            pltpu.VMEM((2, FD, D), BF16),
            gathered,
            gathered,
            pltpu.VMEM((768, D), BF16),
            pltpu.VMEM((512, D), BF16),
            pltpu.VMEM((PEERS, CH, D), BF16),
            pltpu.VMEM((2, 128, 2 * FRAMES), BF16),
            pltpu.VMEM((FRAMES, 768), BF16),
            pltpu.VMEM((2, FRAMES, 256), BF16),
            exchanged,
            exchanged,
            pltpu.VMEM((2, FRAMES + 32, 128), F32),
            exchanged,
            exchanged,
            pltpu.VMEM((2, 8, 128), F32),
            pltpu.VMEM((2, 32, 128), F32),
            pltpu.VMEM((2, 8, 128), F32),
            dma((12,)),
            dma((2, 2, 9)),
            dma((2, 2, 9)),
            dma((2, 2, PEERS)),
            dma((2, 2, PEERS)),
            dma((16,)),
            dma((16,)),
        ],
        compiler_params=pltpu.CompilerParams(
            collective_id=0, has_side_effects=True, vmem_limit_bytes=48 << 20
        ),
    )(
        frames_in, lengths, ln1_gain.reshape(1, D), w_qkv, bias_u, bias_v, pos_keys, w_out,
        ln2_gain.reshape(1, D), w_glu, depth_kernel, bn_scale.reshape(1, D),
        bn_shift.reshape(1, D),
    )


def solution(mesh):
    placed = (
        P("rec", "tm", None),
        P("rec"),
        P(),
        P(None, "tm", None),
        P("tm", None),
        P("tm", None),
        P("tm", None),
        P("tm", None),
        P(),
        P(None, "tm", None),
        P(),
        P(),
        P(),
    )
    return jax.shard_map(
        on_device,
        mesh=mesh,
        in_specs=placed,
        out_specs=(P("rec", "tm", None), P("rec", "tm", None)),
        check_vma=False,
    )
```

time: 429 us -> 113 us (0.26); the launches traced: 423 us -> 112 us
  waiting for transfers between devices: 262 us -> 0 us
  Pallas kernels: 0 us -> 98.2 us
  local copies, waits for them, and re-layouts: 93 us -> 13 us
  matrix products: 31.9 us -> 0 us
  between operations: 14.4 us -> 0.65 us
  starting transfers between devices: 11.8 us -> 0 us
  other arithmetic: 9.71 us -> 0 us
    all_gather x3 -> x0, waiting for transfers between devices: 220 us -> none  [the longest x1 168 us: on_device(): lax.all_gather(w_qkv, 'tm', axis=1, tiled=True)]
    pallas_call x0 -> x1, Pallas kernels: none -> 98.2 us  [on_device(): pl.pallas_call(kernel, out_shape=[jax.ShapeDtypeStruct(frames_in.shape, B...]
    reshape x4, local copies, waits for them, and re-layouts: 40 us -> 2.81 us  [the longest x1 0.7 us: on_device(): ln1_gain.reshape(1, D)]
    all_to_all x2 -> x0, waiting for transfers between devices: 35 us -> none  [the longest x1 18.2 us: on_device(): lax.all_to_all(own_qkv, 'tm', split_axis=3, concat_axis=1, tiled=True)]
    dot_general x10 -> x0, matrix products: 31.9 us -> none  [the longest x1 10.8 us: on_device(): jnp.einsum('rfd,kcd->rfkc', normed, lax.all_gather(w_qkv, 'tm', axis=1, t...]
    slice x17 -> x0, local copies, waits for them, and re-layouts: 27.1 us -> none  [the longest x2 15.1 us: skew_rows(): moved = flat[..., block - 1:block - 1 + block * (width - 1)]]
    all_to_all x2 -> x0, starting transfers between devices: 8.25 us -> none  [the longest x1 4.54 us: on_device(): lax.all_to_all(own_qkv, 'tm', split_axis=3, concat_axis=1, tiled=True)]
    convert_element_type x1 -> x0, local copies, waits for them, and re-layouts: 6.36 us -> none  [on_device(): own_qkv = jnp.einsum('rfd,kcd->rfkc', normed, lax.all_gather(w_qkv, 'tm',...]
  transfers between devices with their start and end apart: 7 -> 0, of which waited for: 6 -> 0; matrix products, arithmetic and copies ran while one was open for 28% -> 0% of each run, Pallas kernels for 0% -> 0%
where the time goes in v1:
time: 113 us; the launch traced here: 112 us
  Pallas kernels  98.2 us (87%)
  local copies, waits for them, and re-layouts  13 us (12%)
    pallas_call x1, Pallas kernels, on_device(): pl.pallas_call(kernel, out_shape=[jax.ShapeDtypeStruct(frames_in.shape, B...  98.2 us
    unnamed x20, local copies, waits for them, and re-layouts  10.2 us

profile of v1, /device:TPU:1, one launch (start us, length us, event | category | flops | bytes accessed | tf_op | source)
XLA Modules:
  0.0 111.8 jit_solution(1745831706407782782)
XLA Ops:
  0.6 0.7 reshape.16.gain1
  1.3 0.7 reshape.17.gain2
  2.0 0.7 reshape.18.scale_ref
  2.7 0.7 reshape.19.shift_ref
  3.4 0.0 copy-start
  3.4 1.5 %copy-done = bf16[3,192,1536]{2,1,0:T(8,128)(2,1)S(1)} copy-done((bf16[3,192,1536]{2,1,0:T(8,128)(2,1)S(1)}, bf16[3,192,1536]{2,1,0:T(8,128)(2,1)}, u32[]{:S(2)}) %copy-start) | copy-done | bytes 1769496
  4.9 0.0 copy-start.1
  4.9 1.3 %copy-done.1 = bf16[2,192,1536]{2,1,0:T(8,128)(2,1)S(1)} copy-done((bf16[2,192,1536]{2,1,0:T(8,128)(2,1)S(1)}, bf16[2,192,1536]{2,1,0:T(8,128)(2,1)}, u32[]{:S(2)}) %copy-start.1) | copy-done | bytes 1179672
  6.2 0.0 copy-start.2
  6.2 1.1 copy-done.2
  7.2 0.0 copy-start.3
  7.3 1.0 copy-done.3
  8.2 0.0 copy-start.4
  8.2 1.0 copy-done.4
  9.2 0.0 copy-start.5
  9.2 0.9 copy-done.5
  10.2 0.0 copy-start.6
  10.2 0.7 copy-done.6
  10.8 0.0 copy-start.7
  10.9 0.7 copy-done.7
  11.5 0.0 copy-start.8
  11.5 0.7 copy-done.8
  12.2 98.2 %shard_map.140 = (bf16[2,64,1536]{2,1,0:T(8,128)(2,1)S(1)}, bf16[2,64,1536]{2,1,0:T(8,128)(2,1)S(1)}) custom-call(bf16[2,64,1536]{2,1,0:T(8,128)(2,1)S(1)} %copy-done.3, s32[2]{0:T(128)S(1)} %copy-done.8, f32[1,1536]{1,0:T(1,128)S(1)} %reshape.16.gain1, bf16[3,192,1536]{2,1,0:T(8,128)(2,1)S(1)} %copy-done, f32[2,96]{1,0:T(2,128)S(1)} %copy-done.6, ...), custom_call_target="tpu_custom_call" | custom-call | tf_op jit(solution)/shard_map/pallas_call | solution.py:387
  110.4 0.7 copy.17
  111.1 0.7 copy.18
Async XLA Ops:
  3.4 1.5 %copy-start = (bf16[3,192,1536]{2,1,0:T(8,128)(2,1)S(1)}, bf16[3,192,1536]{2,1,0:T(8,128)(2,1)}, u32[]{:S(2)}) copy-start(bf16[3,192,1536]{2,1,0:T(8,128)(2,1)} %w_qkv_hbm.1) | copy-start | bytes 5308420
  4.9 1.3 %copy-start.1 = (bf16[2,192,1536]{2,1,0:T(8,128)(2,1)S(1)}, bf16[2,192,1536]{2,1,0:T(8,128)(2,1)}, u32[]{:S(2)}) copy-start(bf16[2,192,1536]{2,1,0:T(8,128)(2,1)} %w_glu_hbm.1) | copy-start | bytes 3538948
  6.2 1.1 copy-start.2
  7.2 1.0 copy-start.3
  8.2 1.0 copy-start.4
  9.2 0.9 copy-start.5
  10.2 0.7 copy-start.6
  10.8 0.7 copy-start.7
  11.5 0.7 copy-start.8

commit v2 on v1

--- a/solution.py
+++ b/solution.py
@@ -39,10 +39,11 @@
 
 
 def kernel(
-    frames_hbm, lengths, gain1, w_qkv_hbm, bias_u, bias_v, pos_hbm, w_out_hbm, gain2, w_glu_hbm,
-    taps_ref, scale_ref, shift_ref,
+    frames_hbm, lengths_hbm, gain1_hbm, w_qkv_hbm, bias_u_hbm, bias_v_hbm, pos_hbm, w_out_hbm,
+    gain2_hbm, w_glu_hbm, taps_hbm, scale_hbm, shift_hbm,
     attended, conv_out,
     x, nrm, n2, wq, wg, wo, pos, qkv, vext, hs, hb, gp, cs, cb, bias_s, taps_s, bn_s,
+    lengths, gain1, bias_u, bias_v, gain2, taps_ref, scale_ref, shift_ref,
     local_sem, ag_send, ag_recv, aa_send, aa_recv, wo_send, wo_recv,
 ):
     rec, me = lax.axis_index("rec"), lax.axis_index("tm")
@@ -72,6 +73,7 @@
     loads = [
         (frames_hbm.at[0], x.at[0]),
         (frames_hbm.at[1], x.at[1]),
+        (gain1_hbm, gain1),
         (w_out_hbm.at[wo_rows, wo_cols], wo.at[me, wo_rows, wo_cols]),
         (w_qkv_hbm.at[0, pl.ds(0, DH)], wq.at[pl.ds(0, DH)]),
         (w_qkv_hbm.at[0, pl.ds(DH, DH)], wq.at[pl.ds(128, DH)]),
@@ -82,6 +84,13 @@
         (pos_hbm.at[pl.ds(DH, DH)], pos.at[1, pl.ds(0, DH)]),
         (w_glu_hbm.at[0], wg.at[pl.ds(0, CH)]),
         (w_glu_hbm.at[1], wg.at[pl.ds(256, CH)]),
+        (lengths_hbm, lengths),
+        (bias_u_hbm, bias_u),
+        (bias_v_hbm, bias_v),
+        (gain2_hbm, gain2),
+        (taps_hbm, taps_ref),
+        (scale_hbm, scale_ref),
+        (shift_hbm, shift_ref),
     ]
     loads = [pltpu.make_async_copy(s, d, local_sem.at[i]) for i, (s, d) in enumerate(loads)]
     for load in loads:
@@ -95,61 +104,63 @@
     for other in (z_up, z_dn, sibling):
         pl.semaphore_signal(barrier, inc=1, device_id=(other, me), device_id_type=MESH)
 
-    def ag(which, buf, r, index, arriving=False):
-        low, high = (pl.ds(0, 32),), (pl.ds(32, 32),)
+    def ag(which, buf, unit, index, arriving=False):
         plan = [
-            (me, (), s_x, s_x),
-            (me, (), s_up, s_dn),
-            (me, (), s_dn, s_up),
-            (s_x, (), s_up, s_dnx),
-            (s_x, (), s_dn, s_upx),
-            (s_dn, low, s_up, s_far),
-            (s_up, high, s_dn, s_far),
-            (s_far, low, s_x, s_farx),
-            (s_far, high, s_x, s_farx),
+            (me, 0, s_x, s_x),
+            (me, 0, s_up, s_dn),
+            (me, 0, s_dn, s_up),
+            (s_x, 0, s_up, s_dnx),
+            (s_x, 0, s_dn, s_upx),
+            (s_dn, 1, s_up, s_far),
+            (s_up, 2, s_dn, s_far),
+            (s_far, 1, s_x, s_farx),
+            (s_far, 2, s_x, s_farx),
         ]
-        src, rows, target, landing = plan[index]
-        sems = (ag_send.at[which, r, index], ag_recv.at[which, r, index])
-        part = buf.at[(r, landing if arriving else src) + rows]
-        return remote(part, part, *sems, (rec, target))
-
-    def ag_start(which, buf, r, *indices):
+        src, part, target, landing = plan[index]
+        rows = pl.ds(unit % 2 * 32 + (16 if part == 2 else 0), 16 if part else 32)
+        frames = buf.at[unit // 2, landing if arriving else src, rows]
+        sems = (ag_send.at[which, unit, index], ag_recv.at[which, unit, index])
+        return remote(frames, frames, *sems, (rec, target))
+
+    def ag_start(which, buf, unit, *indices):
         for index in indices:
-            ag(which, buf, r, index).start()
-
-    def ag_wait(which, buf, r, *indices):
+            ag(which, buf, unit, index).start()
+
+    def ag_wait(which, buf, unit, *indices):
         for index in indices:
-            ag(which, buf, r, index, True).wait_recv()
-
-    def ag_first(which, buf, r):
-        ag_start(which, buf, r, 0, 1, 2)
-
-    def ag_second(which, buf, r):
-        ag_wait(which, buf, r, 1)
-        ag_start(which, buf, r, 5)
-        ag_wait(which, buf, r, 2)
-        ag_start(which, buf, r, 6)
-        ag_wait(which, buf, r, 0)
-        ag_start(which, buf, r, 3, 4)
-
-    def ag_third(which, buf, r):
-        ag_wait(which, buf, r, 5)
-        ag_start(which, buf, r, 7)
-        ag_wait(which, buf, r, 6)
-        ag_start(which, buf, r, 8)
-
-    def ag_finish(which, buf, r):
-        ag_wait(which, buf, r, 3, 4, 7, 8)
+            ag(which, buf, unit, index, True).wait_recv()
+
+    def ag_first(which, buf, *units):
+        for unit in units:
+            ag_start(which, buf, unit, 0, 1, 2)
+
+    def ag_second(which, buf, *units):
+        for unit in units:
+            ag_wait(which, buf, unit, 1)
+            ag_start(which, buf, unit, 5)
+            ag_wait(which, buf, unit, 2)
+            ag_start(which, buf, unit, 6)
+            ag_wait(which, buf, unit, 0)
+            ag_start(which, buf, unit, 3, 4)
+
+    def ag_third(which, buf, *units):
+        for unit in units:
+            ag_wait(which, buf, unit, 5)
+            ag_start(which, buf, unit, 7)
+            ag_wait(which, buf, unit, 6)
+            ag_start(which, buf, unit, 8)
+
+    def ag_finish(which, buf, *units):
+        for unit in units:
+            ag_wait(which, buf, unit, 3, 4, 7, 8)
 
     def aa(which, out, into, r, step, arriving=False):
         to, source = lax.rem(me + step, PEERS), lax.rem(me + PEERS - step, PEERS)
         sems = (aa_send.at[which, r, step], aa_recv.at[which, r, step])
         return remote(out.at[r, to], into.at[r, source if arriving else me], *sems, (rec, to))
 
-    def aa_start(which, out, into, r):
-        for step in range(1, PEERS):
-            aa(which, out, into, r, step).start()
-        into[r, me] = out[r, me]
+    def aa_start(which, out, into, r, step):
+        aa(which, out, into, r, step).start()
 
     def aa_wait(which, out, into, r):
         for step in range(1, PEERS):
@@ -200,7 +211,7 @@
             wo_copy(index, True).wait_recv()
 
     def first_norm(r):
-        nrm[r, me] = norm_rows(x[r].astype(F32), gain1[...])
+        nrm[r, me] = norm_rows(x[r].astype(F32), gain1[...].reshape(1, D))
 
     def project(r):
         rows = nrm.at[r]
@@ -220,8 +231,9 @@
     def attend(r):
         valid = lax.broadcasted_iota(jnp.int32, (128, FRAMES), 1) < lengths[r]
 
-        @pl.loop(0, 4)
-        def _(block):
+        @pl.loop(1, 5)
+        def _(turn):
+            block = lax.rem(y + turn, 4)
             mixed = []
             for h in range(2):
                 q = qkv[pl.ds(pl.multiple_of(block * 128, 128), 128), pl.ds(h * 128, 128)].astype(F32)
@@ -240,6 +252,14 @@
             both = jnp.where(lane < DH, mixed[0], mixed[1])[:, :CH].astype(BF16)
             hs[r, 2 * block] = both[:FD]
             hs[r, 2 * block + 1] = both[FD:]
+            for to in (2 * block, 2 * block + 1):
+                step = lax.rem(to - me + PEERS, PEERS)
+
+                @pl.when(step != 0)
+                def _():
+                    aa_start(0, hs, hb, r, step)
+
+        hb[r, me] = hs[r, me]
 
     def out_project(r):
         heads = jnp.concatenate([hb[r, s] for s in range(PEERS)], axis=-1)
@@ -247,7 +267,7 @@
             cols = pl.ds(n * 512, 512)
             part = dot(heads, wo[:, :, cols].reshape(D, 512))
             attended[r, :, cols] = (x[r, :, cols].astype(F32) + part).astype(BF16)
-        n2[r, me] = norm_rows(attended[r].astype(F32), gain2[...])
+        n2[r, me] = norm_rows(attended[r].astype(F32), gain2[...].reshape(1, D))
 
     def glu(r):
         @pl.loop(0, 4)
@@ -261,19 +281,26 @@
             gp[0, at, :] = gated[:, :128]
             gp[1, at, :] = gated[:, 128:]
 
+    def conv_block(r, block):
+        for c in range(2):
+            total = jnp.zeros((FD, 128), F32)
+            for t in range(TAPS):
+                total += gp[c, pl.ds(block * FD + t + 1, FD), :] * taps_s[c, pl.ds(t, 1), :]
+            s = total * bn_s[0, pl.ds(c, 1), :] + bn_s[1, pl.ds(c, 1), :]
+            out = (s * sigmoid(s)).astype(BF16)
+            if c == 0:
+                cs[r, block, :, pl.ds(0, 128)] = out
+            else:
+                cs[r, block, :, pl.ds(128, 64)] = out[:, :64]
+
     def conv(r):
-        @pl.loop(0, PEERS)
-        def _(block):
-            for c in range(2):
-                total = jnp.zeros((FD, 128), F32)
-                for t in range(TAPS):
-                    total += gp[c, pl.ds(block * FD + t + 1, FD), :] * taps_s[c, pl.ds(t, 1), :]
-                s = total * bn_s[0, pl.ds(c, 1), :] + bn_s[1, pl.ds(c, 1), :]
-                out = (s * sigmoid(s)).astype(BF16)
-                if c == 0:
-                    cs[r, block, :, pl.ds(0, 128)] = out
-                else:
-                    cs[r, block, :, pl.ds(128, 64)] = out[:, :64]
+        @pl.loop(1, PEERS)
+        def _(step):
+            conv_block(r, lax.rem(me + step, PEERS))
+            aa_start(1, cs, cb, r, step)
+
+        conv_block(r, me)
+        cb[r, me] = cs[r, me]
 
     def conv_finish(r):
         conv_out[r] = jnp.concatenate([cb[r, s] for s in range(PEERS)], axis=-1)
@@ -296,7 +323,7 @@
         window = pl.ds(pl.multiple_of((3 * me) // 2 * 128, 128), 256)
 
         def mine(ref, count):
-            part = ref[:, window]
+            part = ref[:, window] if count > 1 else ref[window].reshape(1, 256)
             moved = pltpu.roll(part, 192, 1)
             return jnp.where(jnp.broadcast_to(odd, (count, 256)), moved, part)
 
@@ -309,56 +336,59 @@
             bn_s[1, pl.ds(c, 1), :] = shift[:, cols]
 
     loads[0].wait()
+    loads[2].wait()
     first_norm(0)
     pl.semaphore_wait(barrier, PEERS - 1 + 3)
-    ag_first(0, nrm, 0)
-    loads[2].wait()
-    wo_start(*range(7))
+    ag_first(0, nrm, 0, 1)
     loads[1].wait()
     first_norm(1)
+    ag_first(0, nrm, 2, 3)
+    loads[3].wait()
+    wo_start(*range(7))
+    for load in loads[4:]:
+        load.wait()
     prepare()
-    ag_second(0, nrm, 0)
-    ag_first(0, nrm, 1)
+    ag_second(0, nrm, 0, 1)
     ag_third(0, nrm, 0)
+    ag_second(0, nrm, 2)
+    ag_third(0, nrm, 1)
+    ag_second(0, nrm, 3)
     wo_wait(*range(7))
     wo_start(7, 8, 11)
-    ag_finish(0, nrm, 0)
-    for load in loads[3:]:
-        load.wait()
+    ag_third(0, nrm, 2)
+    ag_finish(0, nrm, 0, 1)
     project(0)
-    ag_second(0, nrm, 1)
+    ag_third(0, nrm, 3)
     attend(0)
-    aa_start(0, hs, hb, 0)
-    ag_third(0, nrm, 1)
+    ag_finish(0, nrm, 2, 3)
+    project(1)
     wo_wait(7)
     wo_start(9, 12)
     wo_wait(8)
     wo_start(10, 13)
-    ag_finish(0, nrm, 1)
-    project(1)
     attend(1)
-    aa_start(0, hs, hb, 1)
     wo_wait(9, 10)
     wo_start(14, 15)
     aa_wait(0, hs, hb, 0)
     wo_wait(*range(11, 16))
     out_project(0)
-    ag_first(1, n2, 0)
+    ag_first(1, n2, 0, 1)
     aa_wait(0, hs, hb, 1)
     out_project(1)
-    ag_second(1, n2, 0)
-    ag_first(1, n2, 1)
+    ag_first(1, n2, 2, 3)
+    ag_second(1, n2, 0, 1)
     ag_third(1, n2, 0)
-    ag_finish(1, n2, 0)
-    ag_second(1, n2, 1)
+    ag_second(1, n2, 2)
+    ag_third(1, n2, 1)
+    ag_second(1, n2, 3)
+    ag_third(1, n2, 2)
+    ag_finish(1, n2, 0, 1)
     glu(0)
+    ag_third(1, n2, 3)
     conv(0)
-    aa_start(1, cs, cb, 0)
-    ag_third(1, n2, 1)
-    ag_finish(1, n2, 1)
+    ag_finish(1, n2, 2, 3)
     glu(1)
     conv(1)
-    aa_start(1, cs, cb, 1)
     aa_wait(1, cs, cb, 0)
     conv_finish(0)
     aa_wait(1, cs, cb, 1)
@@ -366,10 +396,11 @@
 
     for index in range(16):
         wo_copy(index).wait_send()
+    for unit in range(4):
+        for index in range(9):
+            ag(0, nrm, unit, index).wait_send()
+            ag(1, n2, unit, index).wait_send()
     for r in range(2):
-        for index in range(9):
-            ag(0, nrm, r, index).wait_send()
-            ag(1, n2, r, index).wait_send()
         for step in range(1, PEERS):
             aa(0, hs, hb, r, step).wait_send()
             aa(1, cs, cb, r, step).wait_send()
@@ -379,18 +410,14 @@
     frames_in, lengths, ln1_gain, w_qkv, bias_u, bias_v, pos_keys, w_out, ln2_gain, w_glu,
     depth_kernel, bn_scale, bn_shift,
 ):
-    any_space, vmem = pl.BlockSpec(memory_space=pl.ANY), pl.BlockSpec(memory_space=pltpu.VMEM)
-    smem = pl.BlockSpec(memory_space=pltpu.SMEM)
+    vmem = pl.BlockSpec(memory_space=pltpu.VMEM)
     gathered = pltpu.VMEM((2, PEERS, FD, D), BF16)
     exchanged = pltpu.VMEM((2, PEERS, FD, CH), BF16)
     dma = pltpu.SemaphoreType.DMA
     return pl.pallas_call(
         kernel,
         out_shape=[jax.ShapeDtypeStruct(frames_in.shape, BF16)] * 2,
-        in_specs=[
-            any_space, smem, vmem, any_space, vmem, vmem, any_space, any_space, vmem, any_space,
-            vmem, vmem, vmem,
-        ],
+        in_specs=[pl.BlockSpec(memory_space=pl.ANY)] * 13,
         out_specs=[vmem, vmem],
         scratch_shapes=[
             pltpu.VMEM((2, FD, D), BF16),
@@ -410,21 +437,28 @@
             pltpu.VMEM((2, 8, 128), F32),
             pltpu.VMEM((2, 32, 128), F32),
             pltpu.VMEM((2, 8, 128), F32),
-            dma((12,)),
-            dma((2, 2, 9)),
-            dma((2, 2, 9)),
+            pltpu.SMEM((2,), jnp.int32),
+            pltpu.VMEM((D,), F32),
+            pltpu.VMEM((2, DH), F32),
+            pltpu.VMEM((2, DH), F32),
+            pltpu.VMEM((D,), F32),
+            pltpu.VMEM((TAPS, D), F32),
+            pltpu.VMEM((D,), F32),
+            pltpu.VMEM((D,), F32),
+            dma((20,)),
+            dma((2, 4, 9)),
+            dma((2, 4, 9)),
             dma((2, 2, PEERS)),
             dma((2, 2, PEERS)),
             dma((16,)),
             dma((16,)),
         ],
         compiler_params=pltpu.CompilerParams(
-            collective_id=0, has_side_effects=True, vmem_limit_bytes=48 << 20
+            collective_id=0, has_side_effects=True, vmem_limit_bytes=60 << 20
         ),
     )(
-        frames_in, lengths, ln1_gain.reshape(1, D), w_qkv, bias_u, bias_v, pos_keys, w_out,
-        ln2_gain.reshape(1, D), w_glu, depth_kernel, bn_scale.reshape(1, D),
-        bn_shift.reshape(1, D),
+        frames_in, lengths, ln1_gain, w_qkv, bias_u, bias_v, pos_keys, w_out, ln2_gain, w_glu,
+        depth_kernel, bn_scale, bn_shift,
     )
 
 

time: 113 us -> 96.4 us (0.85)
  local copies, waits for them, and re-layouts: 13 us -> 3.53 us
  Pallas kernels: 98.2 us -> 92.1 us
    unnamed x20 -> x2, local copies, waits for them, and re-layouts: 10.2 us -> 3.53 us
    pallas_call x1, Pallas kernels: 98.2 us -> 92.1 us  [on_device(): pl.pallas_call(kernel, out_shape=[jax.ShapeDtypeStruct(frames_in.shape, B...]
    reshape x4 -> x0, local copies, waits for them, and re-layouts: 2.81 us -> none  [the longest x1 0.7 us: on_device(): ln1_gain.reshape(1, D)]
where the time goes in v2:
time: 96.4 us; the launch traced here: 96.3 us
  Pallas kernels  92.1 us (96%)
  local copies, waits for them, and re-layouts  3.53 us (4%)
    pallas_call x1, Pallas kernels, on_device(): pl.pallas_call(kernel, out_shape=[jax.ShapeDtypeStruct(frames_in.shape, B...  92.1 us
    unnamed x2, local copies, waits for them, and re-layouts  3.53 us

profile of v2, /device:TPU:1, one launch (start us, length us, event | category | flops | bytes accessed | tf_op | source)
XLA Modules:
  0.0 96.3 jit_solution(8108090262646086303)
XLA Ops:
  0.6 92.1 %shard_map.140 = (bf16[2,64,1536]{2,1,0:T(8,128)(2,1)}, bf16[2,64,1536]{2,1,0:T(8,128)(2,1)}) custom-call(bf16[2,64,1536]{2,1,0:T(8,128)(2,1)} %frames_hbm.1, s32[2]{0:T(128)} %lengths_hbm.1, f32[1536]{0:T(1024)} %gain1_hbm.1, bf16[3,192,1536]{2,1,0:T(8,128)(2,1)} %w_qkv_hbm.1, f32[2,96]{1,0:T(2,128)} %bias_u_hbm.1, f32[2,96]{1,0:T(2,128)} %bias_v_hbm.1, ...), custom_call_target="tpu_custom_call" | custom-call | tf_op jit(solution)/shard_map/pallas_call | solution.py:417
  92.7 1.8 %copy.17 = bf16[2,64,1536]{2,1,0:T(8,128)(2,1)} copy(bf16[2,64,1536]{2,1,0:T(8,128)(2,1)} %get-tuple-element.4) | data formatting | bytes 786432
  94.5 1.8 %copy.18 = bf16[2,64,1536]{2,1,0:T(8,128)(2,1)} copy(bf16[2,64,1536]{2,1,0:T(8,128)(2,1)} %get-tuple-element.5) | data formatting | bytes 786432

commit v3 on v2

--- a/solution.py
+++ b/solution.py
@@ -82,8 +82,10 @@
         (w_qkv_hbm.at[2], wq.at[pl.ds(512, CH)]),
         (pos_hbm.at[pl.ds(0, DH)], pos.at[0, pl.ds(0, DH)]),
         (pos_hbm.at[pl.ds(DH, DH)], pos.at[1, pl.ds(0, DH)]),
-        (w_glu_hbm.at[0], wg.at[pl.ds(0, CH)]),
-        (w_glu_hbm.at[1], wg.at[pl.ds(256, CH)]),
+        (w_glu_hbm.at[0, pl.ds(0, 128)], wg.at[pl.ds(0, 128)]),
+        (w_glu_hbm.at[1, pl.ds(0, 128)], wg.at[pl.ds(128, 128)]),
+        (w_glu_hbm.at[0, pl.ds(128, 64)], wg.at[pl.ds(256, 64)]),
+        (w_glu_hbm.at[1, pl.ds(128, 64)], wg.at[pl.ds(384, 64)]),
         (lengths_hbm, lengths),
         (bias_u_hbm, bias_u),
         (bias_v_hbm, bias_v),
@@ -213,20 +215,20 @@
     def first_norm(r):
         nrm[r, me] = norm_rows(x[r].astype(F32), gain1[...].reshape(1, D))
 
-    def project(r):
-        rows = nrm.at[r]
+    def project(unit):
+        r, part_rows = unit // 2, pl.ds(unit % 2 * 32, 32)
 
         @pl.loop(0, 3)
         def _(n):
             cols = pl.ds(pl.multiple_of(n * 256, 256), 256)
-            part = dot(rows[...].reshape(FRAMES, D), wq[cols, :], NT)
-            qkv[:, cols] = part.astype(BF16)
-
-        v = qkv[:, pl.ds(512, 256)].astype(F32)
-        lane = lax.broadcasted_iota(jnp.int32, v.shape, 1)
+            part = dot(nrm[r, :, part_rows, :].reshape(256, D), wq[cols, :], NT)
+            qkv[:, part_rows, cols] = part.astype(BF16).reshape(PEERS, 32, 256)
+
+        v = qkv[:, part_rows, pl.ds(512, 256)].astype(F32)
+        lane = lax.broadcasted_iota(jnp.int32, v.shape, 2)
         ones = jnp.where(lane == CH, 1.0, 0.0)
-        vext[0] = jnp.where(lane < DH, v, ones).astype(BF16)
-        vext[1] = jnp.where((lane >= DH) & (lane < CH), v, ones).astype(BF16)
+        vext[0, :, part_rows, :] = jnp.where(lane < DH, v, ones).astype(BF16)
+        vext[1, :, part_rows, :] = jnp.where((lane >= DH) & (lane < CH), v, ones).astype(BF16)
 
     def attend(r):
         valid = lax.broadcasted_iota(jnp.int32, (128, FRAMES), 1) < lengths[r]
@@ -236,17 +238,18 @@
             block = lax.rem(y + turn, 4)
             mixed = []
             for h in range(2):
-                q = qkv[pl.ds(pl.multiple_of(block * 128, 128), 128), pl.ds(h * 128, 128)].astype(F32)
+                q = qkv[pl.ds(2 * block, 2), :, pl.ds(h * 128, 128)].reshape(128, 128).astype(F32)
                 query_u = (q + bias_s[0, pl.ds(h, 1), :]).astype(BF16)
                 query_v = (q + bias_s[1, pl.ds(h, 1), :]).astype(BF16)
-                content = dot(query_u, qkv[:, pl.ds(256 + h * 128, 128)], NT)
+                keys = qkv[:, :, pl.ds(256 + h * 128, 128)].reshape(FRAMES, 128)
+                content = dot(query_u, keys, NT)
                 window = pos[h, :, pl.ds(pl.multiple_of(384 - block * 128, 128), 640)]
                 relative = dot(query_v, window)
                 relative = pltpu.roll(relative, 513, 1, stride=1, stride_axis=0)[:, :FRAMES]
                 scores = jnp.where(valid, content + relative, -1e30)
                 peak = jnp.max(scores, axis=-1, keepdims=True)
                 expd = jnp.exp2((scores - peak) * SCALE2).astype(BF16)
-                out = dot(expd, vext[h])
+                out = dot(expd, vext[h].reshape(FRAMES, 256))
                 mixed.append(out / out[:, CH : CH + 1])
             lane = lax.broadcasted_iota(jnp.int32, mixed[0].shape, 1)
             both = jnp.where(lane < DH, mixed[0], mixed[1])[:, :CH].astype(BF16)
@@ -269,17 +272,19 @@
             attended[r, :, cols] = (x[r, :, cols].astype(F32) + part).astype(BF16)
         n2[r, me] = norm_rows(attended[r].astype(F32), gain2[...].reshape(1, D))
 
-    def glu(r):
-        @pl.loop(0, 4)
-        def _(block):
-            rows = n2[r, pl.ds(block * 2, 2)].reshape(128, D)
-            both = dot(rows, wg[...], NT)
-            gated = both[:, :256] * sigmoid(both[:, 256:])
-            frame = block * 128 + lax.broadcasted_iota(jnp.int32, gated.shape, 0)
+    def glu(unit):
+        r, start = unit // 2, unit % 2 * 32
+
+        @pl.loop(0, 2)
+        def _(c):
+            rows = n2[r, :, pl.ds(start, 32), :].reshape(256, D)
+            both = dot(rows, wg[pl.ds(pl.multiple_of(c * 256, 256), 256), :], NT)
+            gated = (both[:, :128] * sigmoid(both[:, 128:])).reshape(PEERS, 32, 128)
+            frame = lax.broadcasted_iota(jnp.int32, gated.shape, 0) * FD
+            frame += start + lax.broadcasted_iota(jnp.int32, gated.shape, 1)
             gated = jnp.where(frame < lengths[r], gated, 0.0).astype(BF16).astype(F32)
-            at = pl.ds(pl.multiple_of(16 + block * 128, 16), 128)
-            gp[0, at, :] = gated[:, :128]
-            gp[1, at, :] = gated[:, 128:]
+            for s in range(PEERS):
+                gp[c, pl.ds(16 + s * FD + start, 32), :] = gated[s]
 
     def conv_block(r, block):
         for c in range(2):
@@ -309,7 +314,7 @@
         for start in (96, 224, 352, 480):
             wq[pl.ds(start, 32), :] = jnp.zeros((32, D), BF16)
         wq[pl.ds(704, 64), :] = jnp.zeros((64, D), BF16)
-        for start in (192, 448):
+        for start in (320, 448):
             wg[pl.ds(start, 64), :] = jnp.zeros((64, D), BF16)
         for h in range(2):
             pos[h, pl.ds(DH, 32), :] = jnp.zeros((32, 2 * FRAMES), BF16)
@@ -356,12 +361,16 @@
     wo_wait(*range(7))
     wo_start(7, 8, 11)
     ag_third(0, nrm, 2)
-    ag_finish(0, nrm, 0, 1)
+    ag_finish(0, nrm, 0)
     project(0)
+    ag_finish(0, nrm, 1)
+    project(1)
     ag_third(0, nrm, 3)
     attend(0)
-    ag_finish(0, nrm, 2, 3)
-    project(1)
+    ag_finish(0, nrm, 2)
+    project(2)
+    ag_finish(0, nrm, 3)
+    project(3)
     wo_wait(7)
     wo_start(9, 12)
     wo_wait(8)
@@ -382,12 +391,16 @@
     ag_third(1, n2, 1)
     ag_second(1, n2, 3)
     ag_third(1, n2, 2)
-    ag_finish(1, n2, 0, 1)
+    ag_finish(1, n2, 0)
     glu(0)
+    ag_finish(1, n2, 1)
+    glu(1)
     ag_third(1, n2, 3)
     conv(0)
-    ag_finish(1, n2, 2, 3)
-    glu(1)
+    ag_finish(1, n2, 2)
+    glu(2)
+    ag_finish(1, n2, 3)
+    glu(3)
     conv(1)
     aa_wait(1, cs, cb, 0)
     conv_finish(0)
@@ -416,7 +429,7 @@
     dma = pltpu.SemaphoreType.DMA
     return pl.pallas_call(
         kernel,
-        out_shape=[jax.ShapeDtypeStruct(frames_in.shape, BF16)] * 2,
+        out_shape=[pltpu.VMEM(frames_in.shape, BF16)] * 2,
         in_specs=[pl.BlockSpec(memory_space=pl.ANY)] * 13,
         out_specs=[vmem, vmem],
         scratch_shapes=[
@@ -427,8 +440,8 @@
             pltpu.VMEM((512, D), BF16),
             pltpu.VMEM((PEERS, CH, D), BF16),
             pltpu.VMEM((2, 128, 2 * FRAMES), BF16),
-            pltpu.VMEM((FRAMES, 768), BF16),
-            pltpu.VMEM((2, FRAMES, 256), BF16),
+            pltpu.VMEM((PEERS, FD, 768), BF16),
+            pltpu.VMEM((2, PEERS, FD, 256), BF16),
             exchanged,
             exchanged,
             pltpu.VMEM((2, FRAMES + 32, 128), F32),
@@ -445,7 +458,7 @@
             pltpu.VMEM((TAPS, D), F32),
             pltpu.VMEM((D,), F32),
             pltpu.VMEM((D,), F32),
-            dma((20,)),
+            dma((22,)),
             dma((2, 4, 9)),
             dma((2, 4, 9)),
             dma((2, 2, PEERS)),

time: 96.4 us -> 91 us (0.944)
  Pallas kernels: 92.1 us -> 88.8 us
  local copies, waits for them, and re-layouts: 3.53 us -> 1.49 us
    pallas_call x1, Pallas kernels: 92.1 us -> 88.8 us  [on_device(): pl.pallas_call(kernel, out_shape=[pltpu.VMEM(frames_in.shape, BF16)] * 2,...]
    unnamed x2, local copies, waits for them, and re-layouts: 3.53 us -> 1.49 us
where the time goes in v3:
time: 91 us; the launch traced here: 90.9 us
  Pallas kernels  88.8 us (98%)
  local copies, waits for them, and re-layouts  1.49 us (2%)
    pallas_call x1, Pallas kernels, on_device(): pl.pallas_call(kernel, out_shape=[pltpu.VMEM(frames_in.shape, BF16)] * 2,...  88.8 us

profile of v3, /device:TPU:1, one launch (start us, length us, event | category | flops | bytes accessed | tf_op | source)
XLA Modules:
  0.0 90.9 jit_solution(1520939676749246087)
XLA Ops:
  0.6 88.8 %shard_map.140 = (bf16[2,64,1536]{2,1,0:T(8,128)(2,1)S(1)}, bf16[2,64,1536]{2,1,0:T(8,128)(2,1)S(1)}) custom-call(bf16[2,64,1536]{2,1,0:T(8,128)(2,1)} %frames_hbm.1, s32[2]{0:T(128)} %lengths_hbm.1, f32[1536]{0:T(1024)} %gain1_hbm.1, bf16[3,192,1536]{2,1,0:T(8,128)(2,1)} %w_qkv_hbm.1, f32[2,96]{1,0:T(2,128)} %bias_u_hbm.1, f32[2,96]{1,0:T(2,128)} %bias_v_hbm.1, ...), custom_call_target="tpu_custom_call" | custom-call | tf_op jit(solution)/shard_map/pallas_call | solution.py:430
  89.4 0.7 copy.17
  90.2 0.7 copy.18

commit v4 on v3

--- a/solution.py
+++ b/solution.py
@@ -185,10 +185,12 @@
             mine = wo.at[me, wo_rows, wo_cols]
             landed = wo.at[source, wo_rows, wo_cols]
             device = (rec, to)
-        elif index < 11:
+        elif index < 13:
             q_sent, half, q_land, to = [
-                (quarter, None, quarter - 1, z_up),
-                (quarter, None, quarter + 1, z_dn),
+                (quarter, 0, quarter - 1, z_up),
+                (quarter, 1, quarter + 1, z_dn),
+                (quarter, 1, quarter - 1, z_up),
+                (quarter, 0, quarter + 1, z_dn),
                 (quarter - 1, 0, quarter - 2, z_up),
                 (quarter + 1, 1, quarter + 2, z_dn),
             ][index - 7]
@@ -196,9 +198,9 @@
             device = (to, me)
         else:
             q, half = [
-                (quarter, None), (quarter - 1, None), (quarter + 1, None),
-                (quarter - 2, 0), (quarter + 2, 1),
-            ][index - 11]
+                (quarter, None), (quarter - 1, 0), (quarter + 1, 1), (quarter - 1, 1),
+                (quarter + 1, 0), (quarter - 2, 0), (quarter + 2, 1),
+            ][index - 13]
             mine, landed = wo_set(q, core, half), wo_set(q, 1 - core, half)
             device = (sibling, me)
         part = landed if arriving else mine
@@ -359,7 +361,7 @@
     ag_third(0, nrm, 1)
     ag_second(0, nrm, 3)
     wo_wait(*range(7))
-    wo_start(7, 8, 11)
+    wo_start(7, 8, 9, 10, 13)
     ag_third(0, nrm, 2)
     ag_finish(0, nrm, 0)
     project(0)
@@ -372,14 +374,16 @@
     ag_finish(0, nrm, 3)
     project(3)
     wo_wait(7)
-    wo_start(9, 12)
+    wo_start(11, 14)
     wo_wait(8)
-    wo_start(10, 13)
+    wo_start(12, 15)
     attend(1)
     wo_wait(9, 10)
-    wo_start(14, 15)
+    wo_start(16, 17)
+    wo_wait(11, 12)
+    wo_start(18, 19)
     aa_wait(0, hs, hb, 0)
-    wo_wait(*range(11, 16))
+    wo_wait(*range(13, 20))
     out_project(0)
     ag_first(1, n2, 0, 1)
     aa_wait(0, hs, hb, 1)
@@ -407,7 +411,7 @@
     aa_wait(1, cs, cb, 1)
     conv_finish(1)
 
-    for index in range(16):
+    for index in range(20):
         wo_copy(index).wait_send()
     for unit in range(4):
         for index in range(9):
@@ -463,8 +467,8 @@
             dma((2, 4, 9)),
             dma((2, 2, PEERS)),
             dma((2, 2, PEERS)),
-            dma((16,)),
-            dma((16,)),
+            dma((20,)),
+            dma((20,)),
         ],
         compiler_params=pltpu.CompilerParams(
             collective_id=0, has_side_effects=True, vmem_limit_bytes=60 << 20

time: 91 us -> 91.1 us (level)
  no operation moved by 1% of the time
where the time goes in v4:
time: 91.1 us; the launch traced here: 91 us
  Pallas kernels  88.9 us (98%)
  local copies, waits for them, and re-layouts  1.49 us (2%)
    pallas_call x1, Pallas kernels, on_device(): pl.pallas_call(kernel, out_shape=[pltpu.VMEM(frames_in.shape, BF16)] * 2,...  88.9 us

profile of v4, /device:TPU:1, one launch (start us, length us, event | category | flops | bytes accessed | tf_op | source)
XLA Modules:
  0.0 91.0 jit_solution(4096007170577141690)
XLA Ops:
  0.6 88.9 %shard_map.140 = (bf16[2,64,1536]{2,1,0:T(8,128)(2,1)S(1)}, bf16[2,64,1536]{2,1,0:T(8,128)(2,1)S(1)}) custom-call(bf16[2,64,1536]{2,1,0:T(8,128)(2,1)} %frames_hbm.1, s32[2]{0:T(128)} %lengths_hbm.1, f32[1536]{0:T(1024)} %gain1_hbm.1, bf16[3,192,1536]{2,1,0:T(8,128)(2,1)} %w_qkv_hbm.1, f32[2,96]{1,0:T(2,128)} %bias_u_hbm.1, f32[2,96]{1,0:T(2,128)} %bias_v_hbm.1, ...), custom_call_target="tpu_custom_call" | custom-call | tf_op jit(solution)/shard_map/pallas_call | solution.py:434
  89.5 0.7 copy.17
  90.3 0.7 copy.18
